TPU v7x, 512 devices: a whole 4x8x8 slice. The times are simulated.
512 devices in a mesh: rows: 64 (over x, z, core), cols: 8 (over y).
Axes of the slice: x: 4, y: 8, z: 8, core: 2. Of those that a mesh axis runs over, the one named last changes fastest.
Arguments:
- states: float32 [32, 262144], P('cols', 'rows'), may hold values from -120 to 120, as said below
- adj_weight: bfloat16 [2048, 3, 128, 128], P('rows'), may hold values from 0.099609375 to 2
- adj_index: int32 [2048, 3], P('rows'), may hold values from 0 to 2047, as said below
- partner: int32 [2048], P('rows'), may hold values from 0 to 2047, as said below
Outputs:
- correction: float32 [32, 262144], P('cols', 'rows')
Inputs may be any that keep to these rules, and one draw needn't show every extreme that they name: adj_index[b, 0] = b; every other entry lies within 16 blocks of b. partner[partner[b]] = b and partner[b] != b; the 32 blocks of one index of rows have their partners on 32 different other indices of rows, at most one block on each. `states`: finite values.
All inputs are finite; a program needn't handle non-finite values.
Results may differ from a plain program's by a relative error of at most 0.0003.
Values sent between devices are 32-bit elements; how exact they have to be, the bound alone decides.
A program may use at most 64 MiB of HBM per device.

v0:
```python
import jax
import jax.numpy as jnp
from jax import lax
from jax.sharding import PartitionSpec as P

DAMPING = 2.0 / 3.0
EPSILON = 1e-06
EXACT = lax.Precision.HIGHEST


def extended(shard, sides, width):
    for axis, dim in sides:
        peers, length = (lax.axis_size(axis), shard.shape[dim])
        up = [(i, (i + 1) % peers) for i in range(peers - 1)]
        down = [(j, i) for i, j in up]
        last = lax.slice_in_dim(shard, length - width, length, axis=dim)
        initial = lax.slice_in_dim(shard, 0, width, axis=dim)
        before = lax.ppermute(last, axis, up)
        after = lax.ppermute(initial, axis, down)
        shard = jnp.concatenate([before, shard, after], axis=dim)
    return shard


def to_slots(values, owner_dev, row_devices):
    empty = jnp.zeros((values.shape[0], row_devices, values.shape[2]), values.dtype)
    return empty.at[:, owner_dev].set(values)


def from_slots(arrived, owner_dev):
    return arrived[:, owner_dev]


def solve_ritz(gram_matrix, rayleigh):
    factor = jnp.linalg.cholesky(gram_matrix)
    return jax.scipy.linalg.cho_solve((factor, True), rayleigh)


def local(states, adj_weight, adj_index, partner):
    local_cols, vertices = states.shape
    blocks_here = adj_weight.shape[0]
    block_len = adj_weight.shape[2]
    row_devices = lax.axis_size("rows")
    margin_blocks = blocks_here // 2
    local_ids = adj_index - (lax.axis_index("rows") * blocks_here - margin_blocks)
    owner_dev = partner // blocks_here
    degree = jnp.sum(adj_weight, axis=(1, 3), dtype=jnp.float32).reshape(vertices)
    degree_blocks = degree.reshape(1, blocks_here, block_len)

    def operate(vector_in):
        widened = extended(vector_in, (("rows", 1),), margin_blocks * block_len)
        grid_blocks = widened.reshape(local_cols, -1, block_len)
        picked = grid_blocks[:, local_ids]
        neighbour = jnp.einsum(
            "bkij,cbkj->cbi",
            adj_weight,
            picked,
            precision=EXACT,
            preferred_element_type=jnp.float32,
        )
        return degree * vector_in - neighbour.reshape(local_cols, vertices)

    applied = operate(states)
    all_states = lax.all_gather(states, "cols", axis=0, tiled=True)
    gram_part = jnp.einsum("cv,dv->cd", all_states * degree, all_states, precision=EXACT)
    rayleigh_part = jnp.einsum("cv,dv->cd", all_states, applied, precision=EXACT)
    gram_matrix, rayleigh = lax.psum((gram_part, rayleigh_part), "rows")
    ritz_matrix = solve_ritz(gram_matrix, rayleigh)
    residual = applied - degree * jnp.einsum("cd,cv->dv", ritz_matrix, all_states, precision=EXACT)
    presmooth = DAMPING * residual / degree
    remain = (residual - operate(presmooth)).reshape(local_cols, blocks_here, block_len)
    arrived, arrived_degree = (
        lax.all_to_all(
            to_slots(remain, owner_dev, row_devices),
            "rows",
            split_axis=1,
            concat_axis=1,
            tiled=True,
        ),
        lax.all_to_all(
            to_slots(degree_blocks, owner_dev, row_devices),
            "rows",
            split_axis=1,
            concat_axis=1,
            tiled=True,
        ),
    )
    coarse_degree = (degree_blocks + from_slots(arrived_degree, owner_dev)).reshape(vertices)
    coarse = (remain + from_slots(arrived, owner_dev)).reshape(local_cols, vertices)
    coarse_fix = DAMPING * coarse / coarse_degree
    product = operate(coarse_fix).reshape(local_cols, blocks_here, block_len)
    arrived_product = lax.all_to_all(
        to_slots(product, owner_dev, row_devices), "rows", split_axis=1, concat_axis=1, tiled=True
    )
    coarse_image = (product + from_slots(arrived_product, owner_dev)).reshape(local_cols, vertices)
    coarse_fix = coarse_fix + DAMPING * (coarse - coarse_image) / coarse_degree
    second = presmooth + coarse_fix
    smooth = second + DAMPING * (residual - operate(second)) / degree
    squares = lax.psum(jnp.sum(smooth * smooth, axis=1), "rows")
    return smooth / jnp.sqrt(squares / (vertices * row_devices) + EPSILON)[:, None]


def solution(mesh):
    return jax.shard_map(
        local,
        mesh=mesh,
        in_specs=(P("cols", "rows"), P("rows", None, None, None), P("rows", None), P("rows")),
        out_specs=P("cols", "rows"),
        check_vma=False,
    )
```

profile of v0, /device:TPU:1, one launch (start us, length us, event | category | flops | bytes accessed | tf_op | source)
XLA Modules:
  0.0 524.0 jit_solution(13916491231147335106)
XLA Ops:
  0.0 0.8 fusion.27
  0.8 5.4 %collective-permute-start = (f32[4,2048]{1,0:T(4,128)S(1)}, f32[4,2048]{1,0:T(4,128)S(1)}, u32[]{:S(2)}, u32[]{:S(2)}) collective-permute-start(f32[4,2048]{1,0:T(4,128)S(1)} %get-tuple-element.13), channel_id=1, source_target_pairs={{0,8},{8,16},{16,24},{24,32},{32,40},{40,48},{48,56},{56,64},{64,7... | collective-permute-start | bytes 98312 | tf_op jit(solution)/shard_map/ppermute | solution.py:18
  6.2 4.7 collective-permute-start.1
  10.9 0.0 copy-start
  10.9 2.7 convert_reduce_fusion
  13.6 0.0 copy-done.6
  13.6 0.1 copy.22
  13.7 0.1 reshape.73
  13.8 0.0 copy-done.2
  13.8 21.7 %all-gather = f32[8,4,4096]{2,1,0:T(4,128)} all-gather(f32[1,4,4096]{2,1,0:T(4,128)S(1)} %bitcast.137), channel_id=1, replica_groups=mesh['rows'=64,'cols'=8] {'cols'}, dimensions={0}, use_global_device_ids=true | all-gather | bytes 589824 | tf_op jit(solution)/shard_map/all_gather | solution.py:63
  35.6 2.0 reshape.172
  37.6 1.8 fusion.10
  39.4 0.0 copy-start.7
  39.4 0.0 collective-permute-done
  39.4 0.0 collective-permute-done.1
  39.4 0.7 gather_fusion
  40.2 0.0 copy-start.1
  40.2 4.2 fusion.9
  44.4 0.0 copy-done.1
  44.4 0.5 convolution_bitcast_fusion.4
  45.0 251.2 %all-reduce = (f32[32,4]{0,1:T(4,128)S(1)}, f32[32,32]{0,1:T(8,128)S(1)}) all-reduce(f32[32,4]{0,1:T(4,128)S(1)} %convolution_bitcast_fusion.4, f32[32,32]{0,1:T(8,128)S(1)} %fusion.10), channel_id=1, replica_groups=mesh['rows'=64,'cols'=8] {'rows'}, use_global_device_ids=true, to_apply=%region_4.5 | all-reduce | flops 1152 | bytes 9216 | tf_op jit(solution)/shard_map/psum | solution.py:66
  296.1 0.1 copy.24
  296.2 2.9 cholesky.16
  299.2 0.6 compare_reduce_fusion
  299.8 0.7 fusion.16
  300.5 2.4 custom-call.10
  302.9 0.2 fusion.19
  303.1 0.1 fusion.17
  303.2 2.1 multiply_divide_fusion.1
  305.3 3.6 collective-permute-start.2
  308.9 5.2 collective-permute-start.3
  314.2 1.2 scatter_custom_fusion.1
  315.4 4.1 all-to-all-start.1
  319.5 0.0 collective-permute-done.2
  319.5 0.0 collective-permute-done.3
  319.6 0.7 gather_fusion.1
  320.3 4.2 fusion.7
  324.5 0.7 broadcast.105.clone
  325.1 3.6 scatter_fusion
  328.7 0.0 all-to-all-done.1
  328.7 9.9 %all-to-all-start = ((f32[4,64,128]{2,0,1:T(4,128)}), f32[4,64,128]{2,0,1:T(4,128)}, u32[]{:S(2)}, u32[]{:S(2)}) async-start(f32[4,64,128]{2,0,1:T(4,128)} %scatter_fusion), calls=%async_computation | async-start | bytes 262144 | tf_op jit(solution)/shard_map/all_to_all | solution.py:72
  338.6 0.6 gather_fusion.3
  339.2 9.7 %all-to-all-done = f32[4,64,128]{2,0,1:T(4,128)} async-done(((f32[4,64,128]{2,0,1:T(4,128)}), f32[4,64,128]{2,0,1:T(4,128)}, u32[]{:S(2)}, u32[]{:S(2)}) %all-to-all-start) | async-done | bytes 131104 | tf_op jit(solution)/shard_map/all_to_all | solution.py:72
  348.9 1.5 gather_fusion.2
  350.4 0.0 copy-start.5
  350.4 3.2 collective-permute-start.4
  353.7 2.1 collective-permute-start.5
  355.8 0.0 collective-permute-done.4
  355.8 3.1 collective-permute-done.5
  358.9 1.4 gather_fusion.4
  360.3 4.9 fusion.5
  365.2 2.5 scatter_fusion.1
  367.8 18.1 %all_to_all.15 = f32[4,64,128]{2,0,1:T(4,128)} all-to-all(f32[4,64,128]{2,0,1:T(4,128)S(1)} %scatter_fusion.1), channel_id=1, replica_groups=mesh['rows'=64,'cols'=8] {'rows'}, dimensions={1} | all-to-all | bytes 262144 | tf_op jit(solution)/shard_map/all_to_all | solution.py:91
  385.9 1.5 gather_fusion.5
  387.5 0.0 copy-done.3
  387.5 0.9 fusion.13
  388.4 3.2 collective-permute-start.6
  391.7 1.9 collective-permute-start.7
  393.6 0.0 collective-permute-done.6
  393.6 3.3 collective-permute-done.7
  396.9 0.7 gather_fusion.6
  397.6 4.3 multiply_reduce_fusion
  402.0 121.3 %psum.23 = f32[4]{0:T(128)S(1)} all-reduce(f32[4]{0:T(128)S(1)} %get-tuple-element.17), channel_id=1, replica_groups=mesh['rows'=64,'cols'=8] {'rows'}, use_global_device_ids=true, to_apply=%region_9.10 | all-reduce | flops 4 | bytes 32 | tf_op jit(solution)/shard_map/psum | solution.py:98
  523.3 0.7 broadcast_divide_fusion
  (25 shorter events, 0.3 us)
Async XLA Ops:
  0.0 13.8 %copy-start.2 = (f32[4,4096]{1,0:T(4,128)S(1)}, f32[4,4096]{1,0:T(4,128)}, u32[]{:S(2)}) copy-start(f32[4,4096]{1,0:T(4,128)} %param.4) | copy-start | bytes 196612
  0.0 13.6 %copy-start.6 = (s32[32,3]{0,1:T(4,128)S(1)}, s32[32,3]{0,1:T(4,128)}, u32[]{:S(2)}) copy-start(s32[32,3]{0,1:T(4,128)} %param.6) | copy-start | bytes 1156
  0.8 38.5 %collective-permute-start = (f32[4,2048]{1,0:T(4,128)S(1)}, f32[4,2048]{1,0:T(4,128)S(1)}, u32[]{:S(2)}, u32[]{:S(2)}) collective-permute-start(f32[4,2048]{1,0:T(4,128)S(1)} %get-tuple-element.13), channel_id=1, source_target_pairs={{0,8},{8,16},{16,24},{24,32},{32,40},{40,48},{48,56},{56,64},{64,7... | collective-permute-start | bytes 98312 | tf_op jit(solution)/shard_map/ppermute | solution.py:18
  6.2 33.2 %collective-permute-start.1 = (f32[4,2048]{1,0:T(4,128)S(1)}, f32[4,2048]{1,0:T(4,128)S(1)}, u32[]{:S(2)}, u32[]{:S(2)}) collective-permute-start(f32[4,2048]{1,0:T(4,128)S(1)} %get-tuple-element.14), channel_id=1, source_target_pairs={{8,0},{16,8},{24,16},{32,24},{40,32},{48,40},{56,48},{64,56},{72,6... | collective-permute-start | bytes 98312 | tf_op jit(solution)/shard_map/ppermute | solution.py:19
  10.9 29.2 %copy-start = (bf16[32,3,128,128]{3,2,1,0:T(8,128)(2,1)S(1)}, bf16[32,3,128,128]{3,2,1,0:T(8,128)(2,1)}, u32[]{:S(2)}) copy-start(bf16[32,3,128,128]{3,2,1,0:T(8,128)(2,1)} %param.5) | copy-start | bytes 9437188
  39.4 274.8 %copy-start.7 = (s32[32]{0:T(128)S(1)}, s32[32]{0:T(128)}, u32[]{:S(2)}) copy-start(s32[32]{0:T(128)} %param.7) | copy-start | bytes 388
  40.2 4.3 copy-start.1
  305.3 14.2 %collective-permute-start.2 = (f32[4,2048]{1,0:T(4,128)S(1)}, f32[4,2048]{1,0:T(4,128)S(1)}, u32[]{:S(2)}, u32[]{:S(2)}) collective-permute-start(f32[4,2048]{1,0:T(4,128)S(1)} %get-tuple-element.11), channel_id=1, source_target_pairs={{0,8},{8,16},{16,24},{24,32},{32,40},{40,48},{48,56},{56,64},{64,7... | collective-permute-start | bytes 98312 | tf_op jit(solution)/shard_map/ppermute | solution.py:18
  308.9 10.6 %collective-permute-start.3 = (f32[4,2048]{1,0:T(4,128)S(1)}, f32[4,2048]{1,0:T(4,128)S(1)}, u32[]{:S(2)}, u32[]{:S(2)}) collective-permute-start(f32[4,2048]{1,0:T(4,128)S(1)} %get-tuple-element.12), channel_id=1, source_target_pairs={{8,0},{16,8},{24,16},{32,24},{40,32},{48,40},{56,48},{64,56},{72,6... | collective-permute-start | bytes 98312 | tf_op jit(solution)/shard_map/ppermute | solution.py:19
  315.4 13.3 %all-to-all-start.1 = ((f32[1,64,128]{2,0,1:T(1,128)}), f32[1,64,128]{2,0,1:T(1,128)S(1)}, u32[]{:S(2)}, u32[]{:S(2)}) async-start(f32[1,64,128]{2,0,1:T(1,128)} %bitcast.24), calls=%async_computation.1 | async-start | bytes 65536 | tf_op jit(solution)/shard_map/all_to_all | solution.py:79
  324.5 63.0 %copy-start.3 = (f32[4,4096]{1,0:T(4,128)S(1)}, f32[4,4096]{1,0:T(4,128)}, u32[]{:S(2)}) copy-start(f32[4,4096]{1,0:T(4,128)} %get-tuple-element.16) | copy-start | bytes 196612
  328.7 20.1 %all-to-all-start = ((f32[4,64,128]{2,0,1:T(4,128)}), f32[4,64,128]{2,0,1:T(4,128)}, u32[]{:S(2)}, u32[]{:S(2)}) async-start(f32[4,64,128]{2,0,1:T(4,128)} %scatter_fusion), calls=%async_computation | async-start | bytes 262144 | tf_op jit(solution)/shard_map/all_to_all | solution.py:72
  350.4 5.4 %copy-start.5 = (f32[32,4,128]{2,1,0:T(4,128)}, f32[32,4,128]{2,1,0:T(4,128)S(1)}, u32[]{:S(2)}) copy-start(f32[32,4,128]{2,1,0:T(4,128)S(1)} %gather_fusion.2) | copy-start | bytes 196612
  350.4 5.3 %collective-permute-start.4 = (f32[4,2048]{1,0:T(4,128)S(1)}, f32[4,2048]{1,0:T(4,128)S(1)}, u32[]{:S(2)}, u32[]{:S(2)}) collective-permute-start(f32[4,2048]{1,0:T(4,128)S(1)} %get-tuple-element.9), channel_id=1, source_target_pairs={{0,8},{8,16},{16,24},{24,32},{32,40},{40,48},{48,56},{56,64},{64,7... | collective-permute-start | bytes 98312 | tf_op jit(solution)/shard_map/ppermute | solution.py:18
  353.7 5.2 collective-permute-start.5
  388.4 8.5 %copy-start.4 = (f32[4,4096]{1,0:T(4,128)}, f32[4,4096]{1,0:T(4,128)S(1)}, u32[]{:S(2)}) copy-start(f32[4,4096]{1,0:T(4,128)S(1)} %fusion.13) | copy-start | bytes 196612
  388.4 5.2 collective-permute-start.6
  391.7 5.2 collective-permute-start.7
where the time goes:
time: 526 us; the launch traced here: 524 us
  blocking collectives  412 us (78%)
  starting transfers between devices  43.3 us (8%)
  matrix products  22.4 us (4%)
  local copies, waits for them, and re-layouts  18.3 us (3%)
  waiting for transfers between devices  16.1 us (3%)
  other arithmetic  11.2 us (2%)
    psum x1, blocking collectives, local(): gram_matrix, rayleigh = lax.psum((gram_part, rayleigh_part), 'rows')  251 us
    psum x1, blocking collectives, local(): squares = lax.psum(jnp.sum(smooth * smooth, axis=1), 'rows')  121 us
    all_gather x1, blocking collectives, local(): all_states = lax.all_gather(states, 'cols', axis=0, tiled=True)  21.7 us
    all_to_all x1, blocking collectives, local(): lax.all_to_all(to_slots(product, owner_dev, row_devices), 'rows', split_a...  18.1 us
    dot_general x4, matrix products, operate(): jnp.einsum('bkij,cbkj->cbi', adj_weight, picked, precision=EXACT, preferr...  17.7 us
    ppermute x4, starting transfers between devices, extended(): before = lax.ppermute(last, axis, up)  15.4 us
    ppermute x4, starting transfers between devices, extended(): after = lax.ppermute(initial, axis, down)  13.9 us
  transfers between devices with their start and end apart: 10, of which 3 were waited for; matrix products, arithmetic and copies ran while one was open for 3% of the time, Pallas kernels for 0%

commit v1 on v0

v1 whole, which is shorter than its diff:
```python
import jax
import jax.numpy as jnp
from jax import lax
from jax.experimental import pallas as pl
from jax.experimental.pallas import tpu as pltpu
from jax.sharding import PartitionSpec as P

MESH = pl.DeviceIdType.MESH
DAMP = 2.0 / 3.0
EPSILON = 1e-06
F32 = jnp.float32
BF16 = jnp.bfloat16
BLK = 128
NB = 32
HB = 16
NR = 64
NC = 8
COLS = 32
OWN = 4
VERTS = NR * NB * BLK
NT = (((1,), (1,)), ((), ()))


def rcopy(src, dst, send, recv, device):
    return pltpu.make_async_remote_copy(
        src_ref=src, dst_ref=dst, send_sem=send, recv_sem=recv, device_id=device, device_id_type=MESH
    )


def wait_bytes(ref, sem):
    pltpu.make_async_copy(ref, ref, sem).wait()


def parts(x):
    hi = x.astype(BF16).astype(F32)
    rest = x - hi
    mid = rest.astype(BF16).astype(F32)
    return hi, mid, rest - mid


def sum_parts(a):
    return a[0:4] + a[4:8] + a[8:12]


def lanes(shape):
    return lax.broadcasted_iota(jnp.int32, shape, len(shape) - 1)


def kernel(
    states, w_hbm, idx, partner, out,
    wv, ext_y, ext_p, ext_f, ext_s, extp, acc, yg, lparts, deg, appl, resid, remain, cdeg, image, smooth,
    send_d, arr_d, send_r, arr_r, send_i, arr_i, pack_a, pack_b, sq_a, sq_b, slot_v, slot_s,
    w_sem, slot_sem, halo_send, halo_recv, ag_send, ag_recv, pair_send, pair_recv, sum_send, sum_recv,
):
    r = lax.axis_index("rows")
    c = lax.axis_index("cols")
    core = lax.rem(r, 2)
    z = lax.rem(r // 2, 8)
    x = r // 16
    base = r * NB - HB

    def place(b, k):
        return jnp.clip(idx[k, b] - base, 0, NB + 2 * HB - 1)

    loads = [pltpu.make_async_copy(w_hbm.at[:, k], wv.at[k], w_sem.at[k]) for k in range(3)]
    for load in loads:
        load.start()

    barrier = pltpu.get_barrier_semaphore()

    def greet(j, carry):
        pl.semaphore_signal(barrier, inc=1, device_id={"rows": lax.rem(r + j, NR)}, device_id_type=MESH)
        return carry

    lax.fori_loop(1, NR, greet, 0)
    up, down = lax.rem(c + 1, NC), lax.rem(c + NC - 1, NC)
    for peer in (up, down):
        pl.semaphore_signal(barrier, inc=1, device_id={"cols": peer}, device_id_type=MESH)

    for b in range(NB):
        piece = states[:, b * BLK:(b + 1) * BLK]
        ext_y[HB + b] = piece
        yg[c, b] = piece

    lane = lanes((1, 128))
    slot = jnp.zeros((1, 128), jnp.int32)
    for b in range(NB):
        slot = jnp.where(lane == partner[b] // NB, b, slot)
    slot_v[...] = slot
    slot_copy = pltpu.make_async_copy(slot_v, slot_s, slot_sem)
    slot_copy.start()
    for arrived in (arr_d, arr_r, arr_i):
        arrived[r] = jnp.zeros(arrived.shape[1:], F32)
    slot_copy.wait()

    pl.semaphore_wait(barrier, NR - 1 + 2)

    def halo(ext, n):
        left = rcopy(ext.at[pl.ds(HB, HB)], ext.at[pl.ds(HB + NB, HB)], halo_send.at[n, 0], halo_recv.at[n, 0],
                     {"rows": lax.rem(r + NR - 1, NR)})
        right = rcopy(ext.at[pl.ds(NB, HB)], ext.at[pl.ds(0, HB)], halo_send.at[n, 1], halo_recv.at[n, 1],
                      {"rows": lax.rem(r + 1, NR)})
        left.start()
        right.start()
        return left, right

    def gather_step(step):
        copies = []
        if step <= 4:
            block = lax.rem(c + NC - step + 1, NC)
            copies.append(rcopy(yg.at[block], yg.at[block], ag_send.at[0, step - 1], ag_recv.at[0, step - 1], {"cols": up}))
        if step <= 3:
            block = lax.rem(c + step - 1, NC)
            copies.append(rcopy(yg.at[block], yg.at[block], ag_send.at[1, step - 1], ag_recv.at[1, step - 1], {"cols": down}))
        for copy in copies:
            copy.start()
        return copies

    def split_block(ext, j, last):
        hi, mid, lo = parts(ext[j])
        packed = jnp.concatenate([hi, mid, lo, last], axis=0).astype(BF16)
        extp[j] = packed
        return packed

    ones = jnp.ones((OWN, BLK), F32)

    def operate(ext, copies, finish, first=False):
        def own(g, carry):
            for u in range(8):
                b = g * 8 + u
                packed = split_block(ext, HB + b, ones)
                acc[b] = lax.dot_general(packed, wv[0, b], NT, preferred_element_type=F32)
            return carry

        if first:
            loads[0].wait()
        lax.fori_loop(0, NB // 8, own, 0)
        if first:
            loads[1].wait()
            loads[2].wait()
        for copy in copies:
            copy.wait_recv()

        def sides(g, carry):
            for u in range(4):
                split_block(ext, g * 4 + u, ones)
                split_block(ext, HB + NB + g * 4 + u, ones)
            return carry

        lax.fori_loop(0, HB // 4, sides, 0)

        def rest(g, carry):
            for u in range(8):
                b = g * 8 + u
                total = acc[b]
                for k in range(1, 3):
                    total += lax.dot_general(extp[place(b, k)], wv[k, b], NT, preferred_element_type=F32)
                finish(b, sum_parts(total), total[12:16])
            return carry

        lax.fori_loop(0, NB // 8, rest, 0)

    def pair_start(values, send, arrived, n):
        rows = send.shape[1]

        def stage(j, carry):
            send[j] = values[slot_s[0, lax.rem(r + j, NR)]][0:rows]
            return carry

        def go(j, carry):
            rcopy(send.at[j], arrived.at[r], pair_send.at[n], pair_recv.at[n], {"rows": lax.rem(r + j, NR)}).start()
            return carry

        lax.fori_loop(1, NR, stage, 0)
        lax.fori_loop(1, NR, go, 0)

    def pair_wait(arrived, n):
        wait_bytes(arrived.at[pl.ds(0, NR - 1)], pair_recv.at[n])

    def group_sum(value, buf_a, buf_b, n):
        mine = x * 2 + core
        buf_a[mine] = value
        for j in range(1, 8):
            a = lax.rem(mine + j, 8)
            rcopy(buf_a.at[mine], buf_a.at[mine], sum_send.at[n, 0], sum_recv.at[n, 0],
                  {"rows": (a // 2) * 16 + z * 2 + lax.rem(a, 2)}).start()
        wait_bytes(buf_a.at[pl.ds(0, 7)], sum_recv.at[n, 0])
        total = buf_a[0]
        for j in range(1, 8):
            total += buf_a[j]
        buf_b[z] = total
        for j in range(1, 8):
            peer = lax.rem(z + j, 8)
            rcopy(buf_b.at[z], buf_b.at[z], sum_send.at[n, 1], sum_recv.at[n, 1],
                  {"rows": x * 16 + peer * 2 + core}).start()
        wait_bytes(buf_b.at[pl.ds(0, 7)], sum_recv.at[n, 1])
        total = buf_b[0]
        for j in range(1, 8):
            total += buf_b[j]
        return total

    sent = []
    copies = halo(ext_y, 0)
    sent += copies
    steps = gather_step(1)
    sent += steps

    def finish_applied(b, neighbour, degree):
        deg[b] = degree
        appl[b] = degree * ext_y[HB + b] - neighbour

    operate(ext_y, copies, finish_applied, first=True)
    pair_start(deg, send_d, arr_d, 0)
    for step in range(2, 5):
        for copy in steps:
            copy.wait_recv()
        steps = gather_step(step)
        sent += steps
    for copy in steps:
        copy.wait_recv()

    pad = jnp.zeros((16 + 4, BLK), F32)

    def gram(g, total):
        left, right = [], []
        for u in range(2):
            b = g * 2 + u
            block = jnp.concatenate([yg[m, b] for m in range(NC)], axis=0)
            packed = jnp.concatenate(parts(block), axis=0).astype(BF16)
            lparts[b] = packed
            left.append(packed)
            weighted = block * jnp.broadcast_to(deg[b][0:1], (COLS, BLK))
            right.append(jnp.concatenate(parts(weighted) + parts(appl[b]) + (pad,), axis=0).astype(BF16))
        return total + lax.dot_general(
            jnp.concatenate(left, axis=1), jnp.concatenate(right, axis=1), NT, preferred_element_type=F32
        )

    grams = lax.fori_loop(0, NB // 2, gram, jnp.zeros((96, 128), F32))
    grams = grams[0:32] + grams[32:64] + grams[64:96]
    gram_sum = grams + pltpu.roll(grams, 128 - 32, 1) + pltpu.roll(grams, 128 - 64, 1)
    ray_sum = grams + pltpu.roll(grams, 128 - 4, 1) + pltpu.roll(grams, 128 - 8, 1)
    lane = lanes((8, 128))
    offsets = (0, 8, 24, 48)
    packed = jnp.zeros((8, 128), F32)
    for g in range(4):
        piece = jnp.where(lane < 8 * (g + 1), gram_sum[8 * g:8 * g + 8], 0.0)
        packed += pltpu.roll(piece, offsets[g], 1) if offsets[g] else piece
        piece = jnp.where((lane >= 96) & (lane < 100), ray_sum[8 * g:8 * g + 8], 0.0)
        packed += pltpu.roll(piece, 112 + 4 * g, 1)
    packed = group_sum(packed, pack_a, pack_b, 0)
    lower, rhs = [], []
    for g in range(4):
        piece = pltpu.roll(packed, 128 - offsets[g], 1) if offsets[g] else packed
        lower.append(jnp.where(lane < 8 * (g + 1), piece, 0.0))
        rhs.append(jnp.where((lane >= 96) & (lane < 100), pltpu.roll(packed, 16 - 4 * g, 1), 0.0))
    lower = jnp.concatenate(lower, axis=0)
    rhs = jnp.concatenate(rhs, axis=0)
    flipped = jnp.concatenate([lower, jnp.zeros((96, 128), F32)], axis=0).T[0:32]
    lane = lanes((COLS, 128))
    row = lax.broadcasted_iota(jnp.int32, (COLS, 128), 0)
    matrix = jnp.where(lane // 8 <= row // 8, lower, flipped) + rhs

    for k in range(COLS):
        factor = matrix[:, k:k + 1] / matrix[k:k + 1, k:k + 1]
        factor = jnp.where(row[:, 0:1] == k, 0.0, factor)
        matrix = matrix - factor * matrix[k:k + 1, :]
    diagonal = jnp.sum(jnp.where(lane == row, matrix, 0.0), axis=1, keepdims=True)
    ritz = matrix / diagonal
    ritz_t = jnp.concatenate([ritz, jnp.zeros((96, 128), F32)], axis=0).T[96:100]
    mixing = jnp.concatenate(parts(ritz_t) + (jnp.zeros((4, 128), F32),), axis=0)
    mixing = (mixing + pltpu.roll(mixing, 32, 1) + pltpu.roll(mixing, 64, 1))[:, 0:96].astype(BF16)

    def presmooth(g, carry):
        for u in range(8):
            b = g * 8 + u
            mixed = sum_parts(jnp.dot(mixing, lparts[b], preferred_element_type=F32))
            value = appl[b] - deg[b] * mixed
            resid[b] = value
            ext_p[HB + b] = DAMP * value / deg[b]
        return carry

    lax.fori_loop(0, NB // 8, presmooth, 0)
    copies = halo(ext_p, 1)
    sent += copies

    def finish_remain(b, neighbour, _):
        remain[b] = resid[b] - (deg[b] * ext_p[HB + b] - neighbour)

    operate(ext_p, copies, finish_remain)
    pair_start(remain, send_r, arr_r, 1)
    pair_wait(arr_d, 0)
    pair_wait(arr_r, 1)

    def coarse(g, carry):
        for u in range(8):
            b = g * 8 + u
            owner = partner[b] // NB
            total = deg[b] + jnp.broadcast_to(arr_d[owner], (OWN, BLK))
            cdeg[b] = total
            value = remain[b] + arr_r[owner]
            remain[b] = value
            ext_f[HB + b] = DAMP * value / total
        return carry

    lax.fori_loop(0, NB // 8, coarse, 0)
    copies = halo(ext_f, 2)
    sent += copies

    def finish_image(b, neighbour, _):
        image[b] = deg[b] * ext_f[HB + b] - neighbour

    operate(ext_f, copies, finish_image)
    pair_start(image, send_i, arr_i, 2)
    pair_wait(arr_i, 2)

    def second(g, carry):
        for u in range(8):
            b = g * 8 + u
            product = image[b] + arr_i[partner[b] // NB]
            ext_s[HB + b] = ext_p[HB + b] + ext_f[HB + b] + DAMP * (remain[b] - product) / cdeg[b]
        return carry

    lax.fori_loop(0, NB // 8, second, 0)
    copies = halo(ext_s, 3)
    sent += copies

    def finish_smooth(b, neighbour, _):
        value = ext_s[HB + b]
        smooth[b] = value + DAMP * (resid[b] - (deg[b] * value - neighbour)) / deg[b]

    operate(ext_s, copies, finish_smooth)

    squares = jnp.zeros((OWN, BLK), F32)
    for b in range(NB):
        squares += smooth[b] * smooth[b]
    squares = group_sum(squares, sq_a, sq_b, 1)
    scale = lax.rsqrt(jnp.sum(squares, axis=1, keepdims=True) / VERTS + EPSILON)
    for b in range(NB):
        out[:, b * BLK:(b + 1) * BLK] = smooth[b] * scale

    for copy in sent:
        copy.wait_send()
    for n, send in enumerate((send_d, send_r, send_i)):
        wait_bytes(send.at[pl.ds(0, NR - 1)], pair_send.at[n])
    for n, bufs in enumerate(((pack_a, pack_b), (sq_a, sq_b))):
        for half in range(2):
            wait_bytes(bufs[half].at[pl.ds(0, 7)], sum_send.at[n, half])


def local(states, adj_weight, adj_index, partner):
    vmem = pl.BlockSpec(memory_space=pltpu.VMEM)
    smem = pl.BlockSpec(memory_space=pltpu.SMEM)
    field = pltpu.VMEM((NB, OWN, BLK), F32)
    extended = pltpu.VMEM((NB + 2 * HB, OWN, BLK), F32)
    slots = pltpu.VMEM((NR, OWN, BLK), F32)
    slots_d = pltpu.VMEM((NR, 1, BLK), F32)
    dma = pltpu.SemaphoreType.DMA
    return pl.pallas_call(
        kernel,
        out_shape=jax.ShapeDtypeStruct((OWN, NB * BLK), F32),
        in_specs=[vmem, pl.BlockSpec(memory_space=pl.ANY), smem, smem],
        out_specs=vmem,
        scratch_shapes=[
            pltpu.VMEM((3, NB, BLK, BLK), BF16),
            extended, extended, extended, extended,
            pltpu.VMEM((NB + 2 * HB, 16, BLK), BF16),
            pltpu.VMEM((NB, 16, BLK), F32),
            pltpu.VMEM((NC, NB, OWN, BLK), F32),
            pltpu.VMEM((NB, 96, BLK), BF16),
            field, field, field, field, field, field, field,
            slots_d, slots_d, slots, slots, slots, slots,
            pltpu.VMEM((8, 8, 128), F32), pltpu.VMEM((8, 8, 128), F32),
            pltpu.VMEM((8, OWN, 128), F32), pltpu.VMEM((8, OWN, 128), F32),
            pltpu.VMEM((1, 128), jnp.int32), pltpu.SMEM((1, 128), jnp.int32),
            dma((3,)), dma, dma((4, 2)), dma((4, 2)), dma((2, 4)), dma((2, 4)), dma((3,)), dma((3,)),
            dma((2, 2)), dma((2, 2)),
        ],
        compiler_params=pltpu.CompilerParams(
            collective_id=0, has_side_effects=True, vmem_limit_bytes=60 * 1024 * 1024
        ),
        name="precondition",
    )(states, adj_weight, adj_index.T, partner)


def solution(mesh):
    return jax.shard_map(
        local,
        mesh=mesh,
        in_specs=(P("cols", "rows"), P("rows", None, None, None), P("rows", None), P("rows")),
        out_specs=P("cols", "rows"),
        check_vma=False,
    )
```

time: 526 us -> 88.8 us (0.17)
  blocking collectives: 412 us -> 0 us
  Pallas kernels: 0 us -> 87.1 us
  starting transfers between devices: 43.3 us -> 0 us
  matrix products: 22.4 us -> 0 us
  local copies, waits for them, and re-layouts: 18.3 us -> 1.47 us
  waiting for transfers between devices: 16.1 us -> 0 us
  other arithmetic: 11.2 us -> 0 us
    psum x2 -> x0, blocking collectives: 372 us -> none  [the longest x1 251 us: local(): gram_matrix, rayleigh = lax.psum((gram_part, rayleigh_part), 'rows')]
    pallas_call x0 -> x1, Pallas kernels: none -> 87.1 us  [local(): pl.pallas_call(kernel, out_shape=jax.ShapeDtypeStruct((OWN, NB * BLK), F3...]
    ppermute x8 -> x0, starting transfers between devices: 29.4 us -> none  [the longest x4 15.4 us: extended(): before = lax.ppermute(last, axis, up)]
    dot_general x7 -> x0, matrix products: 22.1 us -> none  [the longest x4 17.7 us: operate(): jnp.einsum('bkij,cbkj->cbi', adj_weight, picked, precision=EXACT, preferr...]
    all_gather x1 -> x0, blocking collectives: 21.7 us -> none  [local(): all_states = lax.all_gather(states, 'cols', axis=0, tiled=True)]
    all_to_all x1 -> x0, blocking collectives: 18.1 us -> none  [local(): lax.all_to_all(to_slots(product, owner_dev, row_devices), 'rows', split_a...]
    all_to_all x2 -> x0, starting transfers between devices: 14 us -> none  [the longest x1 9.86 us: local(): lax.all_to_all(to_slots(remain, owner_dev, row_devices), 'rows', split_ax...]
    all_to_all x2 -> x0, waiting for transfers between devices: 9.68 us -> none  [the longest x1 9.68 us: local(): lax.all_to_all(to_slots(remain, owner_dev, row_devices), 'rows', split_ax...]
  transfers between devices with their start and end apart: 10 -> 0, of which waited for: 3 -> 0; matrix products, arithmetic and copies ran while one was open for 3% -> 0% of each run, Pallas kernels for 0% -> 0%
where the time goes in v1:
time: 88.8 us; the launch traced here: 88.6 us
  Pallas kernels  87.1 us (98%)
  local copies, waits for them, and re-layouts  1.47 us (2%)
    pallas_call x1, Pallas kernels, local(): pl.pallas_call(kernel, out_shape=jax.ShapeDtypeStruct((OWN, NB * BLK), F3...  87.1 us

profile of v1, /device:TPU:1, one launch (start us, length us, event | category | flops | bytes accessed | tf_op | source)
XLA Modules:
  0.0 88.6 jit_solution(7852887297812199465)
XLA Ops:
  0.0 87.1 %precondition.1 = f32[4,4096]{1,0:T(4,128)} custom-call(f32[4,4096]{1,0:T(4,128)} %states.1, bf16[32,3,128,128]{3,2,1,0:T(8,128)(2,1)} %w_hbm.1, s32[3,32]{1,0:T(4,128)} %bitcast.1, s32[32]{0:T(128)} %partner.1), custom_call_target="tpu_custom_call" | custom-call | tf_op jit(solution)/shard_map/precondition/pallas_call | solution.py:358
  87.1 1.5 %copy.6 = f32[4,4096]{1,0:T(4,128)} copy(f32[4,4096]{1,0:T(4,128)} %precondition.1) | data formatting | bytes 131072

commit v2 on v1

v2 whole, which is shorter than its diff:
```python
import jax
import jax.numpy as jnp
from jax import lax
from jax.experimental import pallas as pl
from jax.experimental.pallas import tpu as pltpu
from jax.sharding import PartitionSpec as P

MESH = pl.DeviceIdType.MESH
DAMP = 2.0 / 3.0
EPSILON = 1e-06
F32 = jnp.float32
BF16 = jnp.bfloat16
BLK = 128
NB = 32
HB = 16
NR = 64
NC = 8
COLS = 32
PANEL = 4
OWN = 4
VERTS = NR * NB * BLK
NT = (((1,), (1,)), ((), ()))


def rcopy(src, dst, send, recv, device):
    return pltpu.make_async_remote_copy(
        src_ref=src, dst_ref=dst, send_sem=send, recv_sem=recv, device_id=device, device_id_type=MESH
    )


def wait_bytes(ref, sem):
    pltpu.make_async_copy(ref, ref, sem).wait()


def parts(x):
    hi = x.astype(BF16).astype(F32)
    rest = x - hi
    mid = rest.astype(BF16).astype(F32)
    return hi, mid, rest - mid


def sum_parts(a):
    return a[0:4] + a[4:8] + a[8:12]


def lanes(shape):
    return lax.broadcasted_iota(jnp.int32, shape, len(shape) - 1)


def kernel(
    states, w_hbm, idx, partner, out,
    wv, ext_y, ext_z, ext_f, ext_s, extp, acc, deg, appl, fine, coarse, cdeg, image, smooth, pre,
    yt, lt, ct, lparts, mix_out_c, mix_in_c, mix_out_y, mix_in_y,
    send_2, arr_2, send_1, arr_1, send_i, arr_i, pack_c, pack_a, pack_b, sq, slot_v, slot_s,
    w_sem, slot_sem, halo_send, halo_recv, turn_send, turn_recv, pair_send, pair_recv, sum_send, sum_recv,
):
    r = lax.axis_index("rows")
    c = lax.axis_index("cols")
    core = lax.rem(r, 2)
    z = lax.rem(r // 2, 8)
    x = r // 16
    base = r * NB - HB

    def place(b, k):
        return jnp.clip(idx[k, b] - base, 0, NB + 2 * HB - 1)

    loads = [pltpu.make_async_copy(w_hbm.at[:, k], wv.at[k], w_sem.at[k]) for k in range(3)]
    for load in loads:
        load.start()

    barrier = pltpu.get_barrier_semaphore()

    def greet(j, carry):
        pl.semaphore_signal(barrier, inc=1, device_id={"rows": lax.rem(r + j, NR)}, device_id_type=MESH)
        return carry

    for j in range(1, NC):
        pl.semaphore_signal(barrier, inc=1, device_id={"cols": lax.rem(c + j, NC)}, device_id_type=MESH)
    lax.fori_loop(1, NR, greet, 0)

    for b in range(NB):
        ext_y[HB + b] = states[:, b * BLK:(b + 1) * BLK]

    lane = lanes((1, 128))
    slot = jnp.zeros((1, 128), jnp.int32)
    for b in range(NB):
        slot = jnp.where(lane == partner[b] // NB, b, slot)
    slot_v[...] = slot
    slot_copy = pltpu.make_async_copy(slot_v, slot_s, slot_sem)
    slot_copy.start()
    for arrived in (arr_2, arr_1, arr_i):
        arrived[r] = jnp.zeros(arrived.shape[1:], F32)
    slot_copy.wait()

    pl.semaphore_wait(barrier, NR - 1 + NC - 1)

    ends, open_waits = [], {}

    def finish():
        for wait in list(open_waits.values()) + ends:
            wait()

    def halo(ext, n):
        left = rcopy(ext.at[pl.ds(HB, HB)], ext.at[pl.ds(HB + NB, HB)], halo_send.at[n, 0], halo_recv.at[n, 0],
                     {"rows": lax.rem(r + NR - 1, NR)})
        right = rcopy(ext.at[pl.ds(NB, HB)], ext.at[pl.ds(0, HB)], halo_send.at[n, 1], halo_recv.at[n, 1],
                      {"rows": lax.rem(r + 1, NR)})
        left.start()
        right.start()
        ends.extend([left.wait_send, right.wait_send])
        open_waits["halo", n] = lambda: (left.wait_recv(), right.wait_recv())

    def wait(*key):
        open_waits.pop(key)()

    def turn(source, target, n):
        for j in range(1, NC):
            peer = lax.rem(c + j, NC)
            rcopy(source.at[pl.ds(4 * peer, 4)], target.at[pl.ds(4 * c, 4)], turn_send.at[n], turn_recv.at[n],
                  {"cols": peer}).start()
        ends.append(lambda: wait_bytes(target.at[pl.ds(0, 28)], turn_send.at[n]))
        open_waits["turn", n] = lambda: wait_bytes(target.at[pl.ds(0, 28)], turn_recv.at[n])

    ones = jnp.ones((OWN, BLK), F32)

    def split_block(ext, j):
        packed = jnp.concatenate(parts(ext[j]) + (ones,), axis=0).astype(BF16)
        extp[j] = packed
        return packed

    def own_pass(ext):
        def own(g, carry):
            for u in range(8):
                b = g * 8 + u
                acc[b] = lax.dot_general(split_block(ext, HB + b), wv[0, b], NT, preferred_element_type=F32)
            return carry

        lax.fori_loop(0, NB // 8, own, 0)

    def rest_pass(ext, finish_block):
        def sides(g, carry):
            for u in range(4):
                split_block(ext, g * 4 + u)
                split_block(ext, HB + NB + g * 4 + u)
            return carry

        lax.fori_loop(0, HB // 4, sides, 0)

        def rest(g, carry):
            for u in range(8):
                b = g * 8 + u
                total = acc[b]
                for k in range(1, 3):
                    total += lax.dot_general(extp[place(b, k)], wv[k, b], NT, preferred_element_type=F32)
                finish_block(b, sum_parts(total), total[12:16])
            return carry

        lax.fori_loop(0, NB // 8, rest, 0)

    def blocks(step):
        def group(g, carry):
            for u in range(8):
                step(g * 8 + u)
            return carry

        lax.fori_loop(0, NB // 8, group, 0)

    def everyone(source, target, n):
        def go(g, carry):
            for u in range(7):
                j = 1 + g * 7 + u
                rcopy(source(j), target.at[r], pair_send.at[n], pair_recv.at[n], {"rows": lax.rem(r + j, NR)}).start()
            return carry

        lax.fori_loop(0, 9, go, 0)
        ends.append(lambda: wait_bytes(target.at[pl.ds(0, NR - 1)], pair_send.at[n]))
        open_waits["pair", n] = lambda: wait_bytes(target.at[pl.ds(0, NR - 1)], pair_recv.at[n])

    def pair(values, send, arrived, n, extra=None):
        def stage(g, carry):
            for u in range(7):
                j = 1 + g * 7 + u
                block = slot_s[0, lax.rem(r + j, NR)]
                if extra is None:
                    send[j] = values[block]
                else:
                    send[j, 0:OWN] = values[block]
                    send[j, OWN:OWN + 1] = extra[block][0:1]
            return carry

        lax.fori_loop(0, 9, stage, 0)
        everyone(lambda j: send.at[j], arrived, n)

    mine = x * 2 + core

    def sum_start(value, phase):
        buf, place_here, device = (
            (pack_c, c, lambda a: {"cols": a}),
            (pack_a, mine, lambda a: {"rows": (a // 2) * 16 + z * 2 + lax.rem(a, 2)}),
            (pack_b, z, lambda a: {"rows": x * 16 + a * 2 + core}),
        )[phase]
        buf[place_here] = value
        for j in range(1, 8):
            rcopy(buf.at[place_here], buf.at[place_here], sum_send.at[phase], sum_recv.at[phase],
                  device(lax.rem(place_here + j, 8))).start()
        ends.append(lambda: wait_bytes(buf.at[pl.ds(0, 7)], sum_send.at[phase]))
        open_waits["sum", phase] = lambda: wait_bytes(buf.at[pl.ds(0, 7)], sum_recv.at[phase])

    def sum_end(phase):
        buf = (pack_c, pack_a, pack_b)[phase]
        wait("sum", phase)
        return ((buf[0] + buf[1]) + (buf[2] + buf[3])) + ((buf[4] + buf[5]) + (buf[6] + buf[7]))

    halo(ext_y, 0)
    turn(ext_y.at[pl.ds(HB, NB)], yt, 0)
    yt[pl.ds(4 * c, 4)] = ext_y[pl.ds(HB + 4 * c, 4)]
    for load in loads:
        load.wait()
    own_pass(ext_y)
    wait("halo", 0)

    def after_states(b, neighbour, degree):
        mass = degree * ext_y[HB + b]
        deg[b] = degree
        value = mass - neighbour
        appl[b] = value
        ext_z[HB + b] = value / degree
        coarse[b] = (1.0 - DAMP) * mass + DAMP * neighbour

    rest_pass(ext_y, after_states)
    halo(ext_z, 1)
    turn(appl, lt, 1)
    lt[pl.ds(4 * c, 4)] = appl[pl.ds(4 * c, 4)]
    pair(coarse, send_2, arr_2, 0, deg)

    def column(ref, u):
        return jnp.concatenate([ref[4 * m + u] for m in range(NC)], axis=0)

    def packed_parts(block):
        return jnp.concatenate(parts(block), axis=0).astype(BF16)

    wait("turn", 0)
    wait("turn", 1)
    pad = jnp.zeros((32, BLK), BF16)
    left, right_g, right_r = [], [], []
    for u in range(4):
        block = column(yt, u)
        packed = packed_parts(block)
        lparts[u] = packed
        left.append(packed)
        weighted = block * jnp.broadcast_to(deg[4 * c + u][0:1], (COLS, BLK))
        right_g.append(jnp.concatenate([packed_parts(weighted), pad], axis=0))
        right_r.append(jnp.concatenate([packed_parts(column(lt, u)), pad], axis=0))
    left = jnp.concatenate(left, axis=1)
    lane = lanes((8, 128))
    pieces = []
    for right in (right_g, right_r):
        total = lax.dot_general(left, jnp.concatenate(right, axis=1), NT, preferred_element_type=F32)
        total = total[0:32] + total[32:64] + total[64:96]
        total = total + pltpu.roll(total, 128 - 32, 1) + pltpu.roll(total, 128 - 64, 1)
        piece = jnp.where(lane < 32, total[0:8], 0.0)
        for g in range(1, 4):
            piece += pltpu.roll(jnp.where(lane < 32, total[8 * g:8 * g + 8], 0.0), 32 * g, 1)
        pieces.append(piece)
    sum_start(jnp.concatenate(pieces, axis=0), 0)

    own_pass(ext_z)
    sum_start(sum_end(0), 1)
    wait("halo", 1)

    def after_z(b, neighbour, _):
        fine[b] = (1.0 - DAMP) * appl[b] + DAMP * neighbour

    rest_pass(ext_z, after_z)
    sum_start(sum_end(1), 2)
    pair(fine, send_1, arr_1, 1)

    wait("pair", 0)

    def meet(b):
        got = arr_2[partner[b] // NB]
        coarse[b] = coarse[b] + got[0:OWN]
        cdeg[b] = deg[b] + jnp.broadcast_to(got[OWN:OWN + 1], (OWN, BLK))

    blocks(meet)
    turn(coarse, ct, 2)
    ct[pl.ds(4 * c, 4)] = coarse[pl.ds(4 * c, 4)]
    packed = sum_end(2)

    rows_g, rows_r = [], []
    for g in range(4):
        piece = pltpu.roll(packed[0:8], 128 - 32 * g, 1) if g else packed[0:8]
        other = pltpu.roll(packed[8:16], (160 - 32 * g) % 128, 1) if g != 1 else packed[8:16]
        rows_g.append(jnp.where(lane < 32, piece, jnp.where(lane < 64, other, 0.0)))
    matrix = jnp.concatenate(rows_g, axis=0)
    lane32 = lanes((COLS, 128))
    row32 = lax.broadcasted_iota(jnp.int32, (COLS, 128), 0)
    for k in range(0, COLS, PANEL):
        cols_k = [jnp.broadcast_to(matrix[:, k + i:k + i + 1], (COLS, 128)) for i in range(PANEL)]
        rows_k = [matrix[k + i:k + i + 1] for i in range(PANEL)]
        for i in range(PANEL):
            factor = jnp.where(row32 == k + i, 0.0, cols_k[i] * (1.0 / cols_k[i][k + i:k + i + 1]))
            for j in range(i + 1, PANEL):
                cols_k[j] = cols_k[j] - factor * cols_k[j][k + i:k + i + 1]
                rows_k[j] = rows_k[j] - factor[k + j:k + j + 1] * rows_k[i]
            matrix = matrix - factor * rows_k[i]
    diagonal = jnp.sum(jnp.where(lane32 == row32, matrix, 0.0), axis=1, keepdims=True)
    ritz_t = jnp.concatenate([matrix / diagonal, jnp.zeros((96, 128), F32)], axis=0).T[32:64]
    mixing = jnp.concatenate(parts(ritz_t), axis=0)
    mixing = (mixing + pltpu.roll(mixing, 32, 1) + pltpu.roll(mixing, 64, 1))[:, 0:96].astype(BF16)

    def mix(sources, mix_out, mix_in, n):
        wide = jnp.concatenate(sources, axis=1)
        mixed = jnp.dot(mixing, wide, preferred_element_type=F32)
        mixed = mixed[0:32] + mixed[32:64] + mixed[64:96]
        for u in range(4):
            for m in range(NC):
                mix_out[4 * m + u] = mixed[4 * m:4 * m + 4, u * BLK:(u + 1) * BLK]
        turn(mix_out, mix_in, n)
        mix_in[pl.ds(4 * c, 4)] = mix_out[pl.ds(4 * c, 4)]

    wait("turn", 2)
    mix([packed_parts(column(ct, u)) for u in range(4)], mix_out_c, mix_in_c, 3)
    mix([lparts[u] for u in range(4)], mix_out_y, mix_in_y, 4)
    wait("pair", 1)

    def meet_fine(b):
        fine[b] = fine[b] + arr_1[partner[b] // NB]

    blocks(meet_fine)
    wait("turn", 3)

    def fix(b):
        value = fine[b] - mix_in_c[b]
        fine[b] = value
        ext_f[HB + b] = DAMP * value / cdeg[b]

    blocks(fix)
    halo(ext_f, 2)
    own_pass(ext_f)
    wait("halo", 2)

    def after_fix(b, neighbour, _):
        image[b] = deg[b] * ext_f[HB + b] - neighbour

    rest_pass(ext_f, after_fix)
    pair(image, send_i, arr_i, 2)
    wait("turn", 4)

    def prepare(b):
        smoothed = DAMP * (ext_z[HB + b] - mix_in_y[b])
        pre[b] = smoothed
        weight = DAMP / cdeg[b]
        cdeg[b] = weight
        ext_s[HB + b] = smoothed + ext_f[HB + b] + weight * (fine[b] - image[b])

    blocks(prepare)
    wait("pair", 2)

    def second(b):
        ext_s[HB + b] = ext_s[HB + b] - cdeg[b] * arr_i[partner[b] // NB]

    blocks(second)
    halo(ext_s, 3)
    own_pass(ext_s)
    wait("halo", 3)

    def after_second(b, neighbour, _):
        smooth[b] = (1.0 - DAMP) * ext_s[HB + b] + pre[b] + DAMP * neighbour / deg[b]

    rest_pass(ext_s, after_second)

    squares = jnp.zeros((OWN, BLK), F32)
    for b in range(NB):
        squares += smooth[b] * smooth[b]
    squares = jnp.sum(squares, axis=1, keepdims=True)
    lane = lanes((OWN, BLK))
    row = lax.broadcasted_iota(jnp.int32, (OWN, BLK), 0)
    sq[r] = jnp.sum(jnp.where(lane == row, jnp.broadcast_to(squares, (OWN, BLK)), 0.0), axis=0, keepdims=True)
    everyone(lambda j: sq.at[r], sq, 3)
    wait("pair", 3)
    total = jnp.sum(sq[...], axis=0)
    squares = jnp.sum(jnp.where(lane == row, jnp.broadcast_to(total, (OWN, BLK)), 0.0), axis=1, keepdims=True)
    scale = 1.0 / jnp.sqrt(squares / VERTS + EPSILON)
    for b in range(NB):
        out[:, b * BLK:(b + 1) * BLK] = smooth[b] * scale
    finish()


def local(states, adj_weight, adj_index, partner):
    vmem = pl.BlockSpec(memory_space=pltpu.VMEM)
    smem = pl.BlockSpec(memory_space=pltpu.SMEM)
    field = pltpu.VMEM((NB, OWN, BLK), F32)
    extended = pltpu.VMEM((NB + 2 * HB, OWN, BLK), F32)
    slots = pltpu.VMEM((NR, OWN, BLK), F32)
    slots_2 = pltpu.VMEM((NR, OWN + 1, BLK), F32)
    packs = pltpu.VMEM((8, 16, 128), F32)
    dma = pltpu.SemaphoreType.DMA
    return pl.pallas_call(
        kernel,
        out_shape=jax.ShapeDtypeStruct((OWN, NB * BLK), F32),
        in_specs=[vmem, pl.BlockSpec(memory_space=pl.ANY), smem, smem],
        out_specs=vmem,
        scratch_shapes=[
            pltpu.VMEM((3, NB, BLK, BLK), BF16),
            extended, extended, extended, extended,
            pltpu.VMEM((NB + 2 * HB, 16, BLK), BF16),
            pltpu.VMEM((NB, 16, BLK), F32),
            field, field, field, field, field, field, field, field,
            field, field, field,
            pltpu.VMEM((4, 96, BLK), BF16),
            field, field, field, field,
            slots_2, slots_2, slots, slots, slots, slots,
            packs, packs, packs,
            pltpu.VMEM((NR, 1, BLK), F32),
            pltpu.VMEM((1, 128), jnp.int32), pltpu.SMEM((1, 128), jnp.int32),
            dma((3,)), dma, dma((4, 2)), dma((4, 2)), dma((5,)), dma((5,)), dma((4,)), dma((4,)),
            dma((3,)), dma((3,)),
        ],
        compiler_params=pltpu.CompilerParams(
            collective_id=0, has_side_effects=True, vmem_limit_bytes=60 * 1024 * 1024
        ),
        name="precondition",
    )(states, adj_weight, adj_index.T, partner)


def solution(mesh):
    return jax.shard_map(
        local,
        mesh=mesh,
        in_specs=(P("cols", "rows"), P("rows", None, None, None), P("rows", None), P("rows")),
        out_specs=P("cols", "rows"),
        check_vma=False,
    )
```

time: 88.8 us -> 74.6 us (0.84)
  Pallas kernels: 87.1 us -> 72.9 us
    pallas_call x1, Pallas kernels: 87.1 us -> 72.9 us  [local(): pl.pallas_call(kernel, out_shape=jax.ShapeDtypeStruct((OWN, NB * BLK), F3...]
where the time goes in v2:
time: 74.6 us; the launch traced here: 74.4 us
  Pallas kernels  72.9 us (98%)
  local copies, waits for them, and re-layouts  1.47 us (2%)
    pallas_call x1, Pallas kernels, local(): pl.pallas_call(kernel, out_shape=jax.ShapeDtypeStruct((OWN, NB * BLK), F3...  72.9 us

profile of v2, /device:TPU:1, one launch (start us, length us, event | category | flops | bytes accessed | tf_op | source)
XLA Modules:
  0.0 74.4 jit_solution(8881191900884365472)
XLA Ops:
  0.0 72.9 %precondition.1 = f32[4,4096]{1,0:T(4,128)} custom-call(f32[4,4096]{1,0:T(4,128)} %states.1, bf16[32,3,128,128]{3,2,1,0:T(8,128)(2,1)} %w_hbm.1, s32[3,32]{1,0:T(4,128)} %bitcast.1, s32[32]{0:T(128)} %partner.1), custom_call_target="tpu_custom_call" | custom-call | tf_op jit(solution)/shard_map/precondition/pallas_call | solution.py:399
  72.9 1.5 %copy.6 = f32[4,4096]{1,0:T(4,128)} copy(f32[4,4096]{1,0:T(4,128)} %precondition.1) | data formatting | bytes 131072

commit v3 on v2

--- a/solution.py
+++ b/solution.py
@@ -17,6 +17,7 @@
 NC = 8
 COLS = 32
 PANEL = 4
+ORDER = (4, 3, 5, 2, 6, 1, 7)
 OWN = 4
 VERTS = NR * NB * BLK
 NT = (((1,), (1,)), ((), ()))
@@ -48,11 +49,12 @@
 
 
 def kernel(
-    states, w_hbm, idx, partner, out,
+    states_hbm, w_hbm, idx_hbm, partner_hbm, out,
+    states, idx, partner,
     wv, ext_y, ext_z, ext_f, ext_s, extp, acc, deg, appl, fine, coarse, cdeg, image, smooth, pre,
-    yt, lt, ct, lparts, mix_out_c, mix_in_c, mix_out_y, mix_in_y,
+    yt, lt, gathered, ritz_rows, lparts, mix_out_y, mix_in_y,
     send_2, arr_2, send_1, arr_1, send_i, arr_i, pack_c, pack_a, pack_b, sq, slot_v, slot_s,
-    w_sem, slot_sem, halo_send, halo_recv, turn_send, turn_recv, pair_send, pair_recv, sum_send, sum_recv,
+    in_sem, w_sem, slot_sem, halo_send, halo_recv, turn_send, turn_recv, pair_send, pair_recv, sum_send, sum_recv,
 ):
     r = lax.axis_index("rows")
     c = lax.axis_index("cols")
@@ -65,7 +67,9 @@
         return jnp.clip(idx[k, b] - base, 0, NB + 2 * HB - 1)
 
     loads = [pltpu.make_async_copy(w_hbm.at[:, k], wv.at[k], w_sem.at[k]) for k in range(3)]
-    for load in loads:
+    smalls = [pltpu.make_async_copy(a, b, in_sem.at[n]) for n, (a, b) in
+              enumerate(((states_hbm, states), (idx_hbm, idx), (partner_hbm, partner)))]
+    for load in smalls + loads:
         load.start()
 
     barrier = pltpu.get_barrier_semaphore()
@@ -78,6 +82,8 @@
         pl.semaphore_signal(barrier, inc=1, device_id={"cols": lax.rem(c + j, NC)}, device_id_type=MESH)
     lax.fori_loop(1, NR, greet, 0)
 
+    for load in smalls:
+        load.wait()
     for b in range(NB):
         ext_y[HB + b] = states[:, b * BLK:(b + 1) * BLK]
 
@@ -115,7 +121,7 @@
 
     def turn(source, target, n):
         for j in range(1, NC):
-            peer = lax.rem(c + j, NC)
+            peer = lax.rem(c + ORDER[j - 1], NC)
             rcopy(source.at[pl.ds(4 * peer, 4)], target.at[pl.ds(4 * c, 4)], turn_send.at[n], turn_recv.at[n],
                   {"cols": peer}).start()
         ends.append(lambda: wait_bytes(target.at[pl.ds(0, 28)], turn_send.at[n]))
@@ -149,9 +155,9 @@
         def rest(g, carry):
             for u in range(8):
                 b = g * 8 + u
-                total = acc[b]
-                for k in range(1, 3):
-                    total += lax.dot_general(extp[place(b, k)], wv[k, b], NT, preferred_element_type=F32)
+                total = acc[b] + lax.dot_general(
+                    jnp.concatenate([extp[place(b, 1)], extp[place(b, 2)]], axis=1),
+                    jnp.concatenate([wv[1, b], wv[2, b]], axis=1), NT, preferred_element_type=F32)
                 finish_block(b, sum_parts(total), total[12:16])
             return carry
 
@@ -165,30 +171,44 @@
 
         lax.fori_loop(0, NB // 8, group, 0)
 
+    def far_first(g, u):
+        half = (g + 1) // 2
+        to_z = lax.rem(z + 4 + half * (1 - 2 * (g % 2)) + 8, 8)
+        to_x = lax.rem(x + (2, 2, 1, 1, 3, 3, 0, 0)[u], 4)
+        to_core = 1 - core if u % 2 == 0 else core
+        return to_x * 16 + to_z * 2 + to_core
+
     def everyone(source, target, n):
-        def go(g, carry):
-            for u in range(7):
-                j = 1 + g * 7 + u
-                rcopy(source(j), target.at[r], pair_send.at[n], pair_recv.at[n], {"rows": lax.rem(r + j, NR)}).start()
-            return carry
-
-        lax.fori_loop(0, 9, go, 0)
+        def go(g, count):
+            for u in range(count):
+                rcopy(source(g * 8 + u), target.at[r], pair_send.at[n], pair_recv.at[n], {"rows": far_first(g, u)}).start()
+
+        def step(g, carry):
+            go(g, 8)
+            return carry
+
+        lax.fori_loop(0, 7, step, 0)
+        go(7, 7)
         ends.append(lambda: wait_bytes(target.at[pl.ds(0, NR - 1)], pair_send.at[n]))
         open_waits["pair", n] = lambda: wait_bytes(target.at[pl.ds(0, NR - 1)], pair_recv.at[n])
 
     def pair(values, send, arrived, n, extra=None):
-        def stage(g, carry):
-            for u in range(7):
-                j = 1 + g * 7 + u
-                block = slot_s[0, lax.rem(r + j, NR)]
+        def stage(g, count):
+            for u in range(count):
+                j = g * 8 + u
+                block = slot_s[0, far_first(g, u)]
                 if extra is None:
                     send[j] = values[block]
                 else:
                     send[j, 0:OWN] = values[block]
                     send[j, OWN:OWN + 1] = extra[block][0:1]
-            return carry
-
-        lax.fori_loop(0, 9, stage, 0)
+
+        def step(g, carry):
+            stage(g, 8)
+            return carry
+
+        lax.fori_loop(0, 7, step, 0)
+        stage(7, 7)
         everyone(lambda j: send.at[j], arrived, n)
 
     mine = x * 2 + core
@@ -202,7 +222,7 @@
         buf[place_here] = value
         for j in range(1, 8):
             rcopy(buf.at[place_here], buf.at[place_here], sum_send.at[phase], sum_recv.at[phase],
-                  device(lax.rem(place_here + j, 8))).start()
+                  device(lax.rem(place_here + ORDER[j - 1], 8))).start()
         ends.append(lambda: wait_bytes(buf.at[pl.ds(0, 7)], sum_send.at[phase]))
         open_waits["sum", phase] = lambda: wait_bytes(buf.at[pl.ds(0, 7)], sum_recv.at[phase])
 
@@ -232,6 +252,14 @@
     turn(appl, lt, 1)
     lt[pl.ds(4 * c, 4)] = appl[pl.ds(4 * c, 4)]
     pair(coarse, send_2, arr_2, 0, deg)
+    own_pass(ext_z)
+    wait("halo", 1)
+
+    def after_z(b, neighbour, _):
+        fine[b] = (1.0 - DAMP) * appl[b] + DAMP * neighbour
+
+    rest_pass(ext_z, after_z)
+    pair(fine, send_1, arr_1, 1)
 
     def column(ref, u):
         return jnp.concatenate([ref[4 * m + u] for m in range(NC)], axis=0)
@@ -264,27 +292,29 @@
         pieces.append(piece)
     sum_start(jnp.concatenate(pieces, axis=0), 0)
 
-    own_pass(ext_z)
     sum_start(sum_end(0), 1)
-    wait("halo", 1)
-
-    def after_z(b, neighbour, _):
-        fine[b] = (1.0 - DAMP) * appl[b] + DAMP * neighbour
-
-    rest_pass(ext_z, after_z)
-    sum_start(sum_end(1), 2)
-    pair(fine, send_1, arr_1, 1)
-
     wait("pair", 0)
 
     def meet(b):
         got = arr_2[partner[b] // NB]
-        coarse[b] = coarse[b] + got[0:OWN]
+        value = coarse[b] + got[0:OWN]
+        coarse[b] = value
+        gathered[c, b] = value
         cdeg[b] = deg[b] + jnp.broadcast_to(got[OWN:OWN + 1], (OWN, BLK))
 
     blocks(meet)
-    turn(coarse, ct, 2)
-    ct[pl.ds(4 * c, 4)] = coarse[pl.ds(4 * c, 4)]
+    for j in range(1, NC):
+        peer = lax.rem(c + ORDER[j - 1], NC)
+        rcopy(coarse, gathered.at[c], turn_send.at[2], turn_recv.at[2], {"cols": peer}).start()
+    ends.append(lambda: wait_bytes(gathered.at[pl.ds(0, 7)], turn_send.at[2]))
+    open_waits["turn", 2] = lambda: wait_bytes(gathered.at[pl.ds(0, 7)], turn_recv.at[2])
+    sum_start(sum_end(1), 2)
+    wait("pair", 1)
+
+    def meet_fine(b):
+        fine[b] = fine[b] + arr_1[partner[b] // NB]
+
+    blocks(meet_fine)
     packed = sum_end(2)
 
     rows_g, rows_r = [], []
@@ -319,19 +349,16 @@
         turn(mix_out, mix_in, n)
         mix_in[pl.ds(4 * c, 4)] = mix_out[pl.ds(4 * c, 4)]
 
+    for m in range(NC):
+        ritz_rows[m] = ritz_t[4 * m:4 * m + 4]
+    mixing_own = jnp.concatenate(parts(ritz_rows[c]) + (jnp.zeros((OWN, 128), F32),), axis=0)
+    mixing_own = (mixing_own + pltpu.roll(mixing_own, 32, 1) + pltpu.roll(mixing_own, 64, 1))[:, 0:96].astype(BF16)
     wait("turn", 2)
-    mix([packed_parts(column(ct, u)) for u in range(4)], mix_out_c, mix_in_c, 3)
-    mix([lparts[u] for u in range(4)], mix_out_y, mix_in_y, 4)
-    wait("pair", 1)
-
-    def meet_fine(b):
-        fine[b] = fine[b] + arr_1[partner[b] // NB]
-
-    blocks(meet_fine)
-    wait("turn", 3)
 
     def fix(b):
-        value = fine[b] - mix_in_c[b]
+        column_b = jnp.concatenate([gathered[m, b] for m in range(NC)], axis=0)
+        mixed = jnp.dot(mixing_own, packed_parts(column_b), preferred_element_type=F32)
+        value = fine[b] - sum_parts(mixed)
         fine[b] = value
         ext_f[HB + b] = DAMP * value / cdeg[b]
 
@@ -345,6 +372,7 @@
 
     rest_pass(ext_f, after_fix)
     pair(image, send_i, arr_i, 2)
+    mix([lparts[u] for u in range(4)], mix_out_y, mix_in_y, 4)
     wait("turn", 4)
 
     def prepare(b):
@@ -389,7 +417,6 @@
 
 def local(states, adj_weight, adj_index, partner):
     vmem = pl.BlockSpec(memory_space=pltpu.VMEM)
-    smem = pl.BlockSpec(memory_space=pltpu.SMEM)
     field = pltpu.VMEM((NB, OWN, BLK), F32)
     extended = pltpu.VMEM((NB + 2 * HB, OWN, BLK), F32)
     slots = pltpu.VMEM((NR, OWN, BLK), F32)
@@ -399,22 +426,24 @@
     return pl.pallas_call(
         kernel,
         out_shape=jax.ShapeDtypeStruct((OWN, NB * BLK), F32),
-        in_specs=[vmem, pl.BlockSpec(memory_space=pl.ANY), smem, smem],
+        in_specs=[pl.BlockSpec(memory_space=pltpu.HBM)] * 4,
         out_specs=vmem,
         scratch_shapes=[
+            pltpu.VMEM((OWN, NB * BLK), F32), pltpu.SMEM((3, NB), jnp.int32), pltpu.SMEM((NB,), jnp.int32),
             pltpu.VMEM((3, NB, BLK, BLK), BF16),
             extended, extended, extended, extended,
             pltpu.VMEM((NB + 2 * HB, 16, BLK), BF16),
             pltpu.VMEM((NB, 16, BLK), F32),
             field, field, field, field, field, field, field, field,
-            field, field, field,
+            field, field,
+            pltpu.VMEM((NC, NB, OWN, BLK), F32), pltpu.VMEM((NC, OWN, 128), F32),
             pltpu.VMEM((4, 96, BLK), BF16),
-            field, field, field, field,
+            field, field,
             slots_2, slots_2, slots, slots, slots, slots,
             packs, packs, packs,
             pltpu.VMEM((NR, 1, BLK), F32),
             pltpu.VMEM((1, 128), jnp.int32), pltpu.SMEM((1, 128), jnp.int32),
-            dma((3,)), dma, dma((4, 2)), dma((4, 2)), dma((5,)), dma((5,)), dma((4,)), dma((4,)),
+            dma((3,)), dma((3,)), dma, dma((4, 2)), dma((4, 2)), dma((5,)), dma((5,)), dma((4,)), dma((4,)),
             dma((3,)), dma((3,)),
         ],
         compiler_params=pltpu.CompilerParams(

time: 74.6 us -> 68.2 us (0.914)
  Pallas kernels: 72.9 us -> 66.6 us
    pallas_call x1, Pallas kernels: 72.9 us -> 66.6 us  [local(): pl.pallas_call(kernel, out_shape=jax.ShapeDtypeStruct((OWN, NB * BLK), F3...]
where the time goes in v3:
time: 68.2 us; the launch traced here: 68.1 us
  Pallas kernels  66.6 us (98%)
  local copies, waits for them, and re-layouts  1.47 us (2%)
    pallas_call x1, Pallas kernels, local(): pl.pallas_call(kernel, out_shape=jax.ShapeDtypeStruct((OWN, NB * BLK), F3...  66.6 us
    unnamed x1, local copies, waits for them, and re-layouts  1.47 us

profile of v3, /device:TPU:1, one launch (start us, length us, event | category | flops | bytes accessed | tf_op | source)
XLA Modules:
  0.0 68.1 jit_solution(15277353436241406787)
XLA Ops:
  0.0 66.6 %precondition.1 = f32[4,4096]{1,0:T(4,128)} custom-call(f32[4,4096]{1,0:T(4,128)} %states_hbm.1, bf16[32,3,128,128]{3,2,1,0:T(8,128)(2,1)} %w_hbm.1, s32[3,32]{1,0:T(4,128)} %bitcast.1, s32[32]{0:T(128)} %partner_hbm.1), custom_call_target="tpu_custom_call" | custom-call | tf_op jit(solution)/shard_map/precondition/pallas_call | solution.py:426
  66.6 1.5 %copy.6 = f32[4,4096]{1,0:T(4,128)} copy(f32[4,4096]{1,0:T(4,128)} %precondition.1) | data formatting | bytes 131072

commit v4 on v3

--- a/solution.py
+++ b/solution.py
@@ -75,7 +75,7 @@
     barrier = pltpu.get_barrier_semaphore()
 
     def greet(j, carry):
-        pl.semaphore_signal(barrier, inc=1, device_id={"rows": lax.rem(r + j, NR)}, device_id_type=MESH)
+        pl.semaphore_signal(barrier, inc=1, device_id={"rows": lax.rem(r + NR // 2 + j, NR)}, device_id_type=MESH)
         return carry
 
     for j in range(1, NC):
@@ -135,41 +135,22 @@
         return packed
 
     def own_pass(ext):
-        def own(g, carry):
-            for u in range(8):
-                b = g * 8 + u
-                acc[b] = lax.dot_general(split_block(ext, HB + b), wv[0, b], NT, preferred_element_type=F32)
-            return carry
-
-        lax.fori_loop(0, NB // 8, own, 0)
+        for b in range(NB):
+            acc[b] = lax.dot_general(split_block(ext, HB + b), wv[0, b], NT, preferred_element_type=F32)
 
     def rest_pass(ext, finish_block):
-        def sides(g, carry):
-            for u in range(4):
-                split_block(ext, g * 4 + u)
-                split_block(ext, HB + NB + g * 4 + u)
-            return carry
-
-        lax.fori_loop(0, HB // 4, sides, 0)
-
-        def rest(g, carry):
-            for u in range(8):
-                b = g * 8 + u
-                total = acc[b] + lax.dot_general(
-                    jnp.concatenate([extp[place(b, 1)], extp[place(b, 2)]], axis=1),
-                    jnp.concatenate([wv[1, b], wv[2, b]], axis=1), NT, preferred_element_type=F32)
-                finish_block(b, sum_parts(total), total[12:16])
-            return carry
-
-        lax.fori_loop(0, NB // 8, rest, 0)
+        for j in range(HB):
+            split_block(ext, j)
+            split_block(ext, HB + NB + j)
+        for b in range(NB):
+            total = acc[b] + lax.dot_general(
+                jnp.concatenate([extp[place(b, 1)], extp[place(b, 2)]], axis=1),
+                jnp.concatenate([wv[1, b], wv[2, b]], axis=1), NT, preferred_element_type=F32)
+            finish_block(b, sum_parts(total), total[12:16])
 
     def blocks(step):
-        def group(g, carry):
-            for u in range(8):
-                step(g * 8 + u)
-            return carry
-
-        lax.fori_loop(0, NB // 8, group, 0)
+        for b in range(NB):
+            step(b)
 
     def far_first(g, u):
         half = (g + 1) // 2
@@ -251,16 +232,8 @@
     halo(ext_z, 1)
     turn(appl, lt, 1)
     lt[pl.ds(4 * c, 4)] = appl[pl.ds(4 * c, 4)]
-    pair(coarse, send_2, arr_2, 0, deg)
+    pair(coarse, send_2, arr_2, 0)
     own_pass(ext_z)
-    wait("halo", 1)
-
-    def after_z(b, neighbour, _):
-        fine[b] = (1.0 - DAMP) * appl[b] + DAMP * neighbour
-
-    rest_pass(ext_z, after_z)
-    pair(fine, send_1, arr_1, 1)
-
     def column(ref, u):
         return jnp.concatenate([ref[4 * m + u] for m in range(NC)], axis=0)
 
@@ -291,16 +264,22 @@
             piece += pltpu.roll(jnp.where(lane < 32, total[8 * g:8 * g + 8], 0.0), 32 * g, 1)
         pieces.append(piece)
     sum_start(jnp.concatenate(pieces, axis=0), 0)
+    wait("halo", 1)
+
+    def after_z(b, neighbour, _):
+        fine[b] = (1.0 - DAMP) * appl[b] + DAMP * neighbour
+
+    rest_pass(ext_z, after_z)
+    pair(fine, send_1, arr_1, 1, deg)
+
 
     sum_start(sum_end(0), 1)
     wait("pair", 0)
 
     def meet(b):
-        got = arr_2[partner[b] // NB]
-        value = coarse[b] + got[0:OWN]
+        value = coarse[b] + arr_2[partner[b] // NB]
         coarse[b] = value
         gathered[c, b] = value
-        cdeg[b] = deg[b] + jnp.broadcast_to(got[OWN:OWN + 1], (OWN, BLK))
 
     blocks(meet)
     for j in range(1, NC):
@@ -312,7 +291,9 @@
     wait("pair", 1)
 
     def meet_fine(b):
-        fine[b] = fine[b] + arr_1[partner[b] // NB]
+        got = arr_1[partner[b] // NB]
+        fine[b] = fine[b] + got[0:OWN]
+        cdeg[b] = DAMP / (deg[b] + jnp.broadcast_to(got[OWN:OWN + 1], (OWN, BLK)))
 
     blocks(meet_fine)
     packed = sum_end(2)
@@ -360,7 +341,7 @@
         mixed = jnp.dot(mixing_own, packed_parts(column_b), preferred_element_type=F32)
         value = fine[b] - sum_parts(mixed)
         fine[b] = value
-        ext_f[HB + b] = DAMP * value / cdeg[b]
+        ext_f[HB + b] = value * cdeg[b]
 
     blocks(fix)
     halo(ext_f, 2)
@@ -378,9 +359,7 @@
     def prepare(b):
         smoothed = DAMP * (ext_z[HB + b] - mix_in_y[b])
         pre[b] = smoothed
-        weight = DAMP / cdeg[b]
-        cdeg[b] = weight
-        ext_s[HB + b] = smoothed + ext_f[HB + b] + weight * (fine[b] - image[b])
+        ext_s[HB + b] = smoothed + ext_f[HB + b] + cdeg[b] * (fine[b] - image[b])
 
     blocks(prepare)
     wait("pair", 2)
@@ -439,7 +418,7 @@
             pltpu.VMEM((NC, NB, OWN, BLK), F32), pltpu.VMEM((NC, OWN, 128), F32),
             pltpu.VMEM((4, 96, BLK), BF16),
             field, field,
-            slots_2, slots_2, slots, slots, slots, slots,
+            slots, slots, slots_2, slots_2, slots, slots,
             packs, packs, packs,
             pltpu.VMEM((NR, 1, BLK), F32),
             pltpu.VMEM((1, 128), jnp.int32), pltpu.SMEM((1, 128), jnp.int32),

time: 68.2 us -> 65.7 us (0.963)
  Pallas kernels: 66.6 us -> 64.1 us
    pallas_call x1, Pallas kernels: 66.6 us -> 64.1 us  [local(): pl.pallas_call(kernel, out_shape=jax.ShapeDtypeStruct((OWN, NB * BLK), F3...]
where the time goes in v4:
time: 65.7 us; the launch traced here: 65.5 us
  Pallas kernels  64.1 us (98%)
  local copies, waits for them, and re-layouts  1.47 us (2%)
    pallas_call x1, Pallas kernels, local(): pl.pallas_call(kernel, out_shape=jax.ShapeDtypeStruct((OWN, NB * BLK), F3...  64.1 us
    unnamed x1, local copies, waits for them, and re-layouts  1.47 us

profile of v4, /device:TPU:1, one launch (start us, length us, event | category | flops | bytes accessed | tf_op | source)
XLA Modules:
  0.0 65.5 jit_solution(13958087014678442387)
XLA Ops:
  0.0 64.1 %precondition.1 = f32[4,4096]{1,0:T(4,128)} custom-call(f32[4,4096]{1,0:T(4,128)} %states_hbm.1, bf16[32,3,128,128]{3,2,1,0:T(8,128)(2,1)} %w_hbm.1, s32[3,32]{1,0:T(4,128)} %bitcast.1, s32[32]{0:T(128)} %partner_hbm.1), custom_call_target="tpu_custom_call" | custom-call | tf_op jit(solution)/shard_map/precondition/pallas_call | solution.py:405
  64.1 1.5 %copy.6 = f32[4,4096]{1,0:T(4,128)} copy(f32[4,4096]{1,0:T(4,128)} %precondition.1) | data formatting | bytes 131072

commit v5 on v4

--- a/solution.py
+++ b/solution.py
@@ -16,7 +16,7 @@
 NR = 64
 NC = 8
 COLS = 32
-PANEL = 4
+PANEL = 8
 ORDER = (4, 3, 5, 2, 6, 1, 7)
 OWN = 4
 VERTS = NR * NB * BLK
@@ -66,38 +66,27 @@
     def place(b, k):
         return jnp.clip(idx[k, b] - base, 0, NB + 2 * HB - 1)
 
-    loads = [pltpu.make_async_copy(w_hbm.at[:, k], wv.at[k], w_sem.at[k]) for k in range(3)]
+    barrier = pltpu.get_barrier_semaphore()
+
+    def greet_rows(g, carry):
+        for u in range(7):
+            ahead = NR // 2 + g * 7 + u
+            ahead = ahead + jnp.where(ahead >= NR, 1, 0)
+            pl.semaphore_signal(barrier, inc=1, device_id={"rows": lax.rem(r + ahead, NR)}, device_id_type=MESH)
+        return carry
+
     smalls = [pltpu.make_async_copy(a, b, in_sem.at[n]) for n, (a, b) in
               enumerate(((states_hbm, states), (idx_hbm, idx), (partner_hbm, partner)))]
-    for load in smalls + loads:
+    smalls[0].start()
+    for ahead in ORDER:
+        pl.semaphore_signal(barrier, inc=1, device_id={"cols": lax.rem(c + ahead, NC)}, device_id_type=MESH)
+    lax.fori_loop(0, 9, greet_rows, 0)
+    loads = [pltpu.make_async_copy(w_hbm.at[:, k], wv.at[k], w_sem.at[k]) for k in range(3)]
+    for load in smalls[1:] + loads:
         load.start()
-
-    barrier = pltpu.get_barrier_semaphore()
-
-    def greet(j, carry):
-        pl.semaphore_signal(barrier, inc=1, device_id={"rows": lax.rem(r + NR // 2 + j, NR)}, device_id_type=MESH)
-        return carry
-
-    for j in range(1, NC):
-        pl.semaphore_signal(barrier, inc=1, device_id={"cols": lax.rem(c + j, NC)}, device_id_type=MESH)
-    lax.fori_loop(1, NR, greet, 0)
-
-    for load in smalls:
-        load.wait()
+    smalls[0].wait()
     for b in range(NB):
         ext_y[HB + b] = states[:, b * BLK:(b + 1) * BLK]
-
-    lane = lanes((1, 128))
-    slot = jnp.zeros((1, 128), jnp.int32)
-    for b in range(NB):
-        slot = jnp.where(lane == partner[b] // NB, b, slot)
-    slot_v[...] = slot
-    slot_copy = pltpu.make_async_copy(slot_v, slot_s, slot_sem)
-    slot_copy.start()
-    for arrived in (arr_2, arr_1, arr_i):
-        arrived[r] = jnp.zeros(arrived.shape[1:], F32)
-    slot_copy.wait()
-
     pl.semaphore_wait(barrier, NR - 1 + NC - 1)
 
     ends, open_waits = [], {}
@@ -215,9 +204,22 @@
     halo(ext_y, 0)
     turn(ext_y.at[pl.ds(HB, NB)], yt, 0)
     yt[pl.ds(4 * c, 4)] = ext_y[pl.ds(HB + 4 * c, 4)]
-    for load in loads:
+    loads[0].wait()
+    own_pass(ext_y)
+
+    for load in smalls[1:]:
         load.wait()
-    own_pass(ext_y)
+    lane = lanes((1, 128))
+    slot = jnp.zeros((1, 128), jnp.int32)
+    for b in range(NB):
+        slot = jnp.where(lane == partner[b] // NB, b, slot)
+    slot_v[...] = slot
+    slot_copy = pltpu.make_async_copy(slot_v, slot_s, slot_sem)
+    slot_copy.start()
+    for arrived in (arr_2, arr_1, arr_i):
+        arrived[r] = jnp.zeros(arrived.shape[1:], F32)
+    for load in loads[1:]:
+        load.wait()
     wait("halo", 0)
 
     def after_states(b, neighbour, degree):
@@ -231,6 +233,7 @@
     rest_pass(ext_y, after_states)
     halo(ext_z, 1)
     turn(appl, lt, 1)
+    slot_copy.wait()
     lt[pl.ds(4 * c, 4)] = appl[pl.ds(4 * c, 4)]
     pair(coarse, send_2, arr_2, 0)
     own_pass(ext_z)
@@ -273,7 +276,6 @@
     pair(fine, send_1, arr_1, 1, deg)
 
 
-    sum_start(sum_end(0), 1)
     wait("pair", 0)
 
     def meet(b):
@@ -287,6 +289,7 @@
         rcopy(coarse, gathered.at[c], turn_send.at[2], turn_recv.at[2], {"cols": peer}).start()
     ends.append(lambda: wait_bytes(gathered.at[pl.ds(0, 7)], turn_send.at[2]))
     open_waits["turn", 2] = lambda: wait_bytes(gathered.at[pl.ds(0, 7)], turn_recv.at[2])
+    sum_start(sum_end(0), 1)
     sum_start(sum_end(1), 2)
     wait("pair", 1)
 

time: 65.7 us -> 64.3 us (0.979)
  Pallas kernels: 64.1 us -> 62.7 us
    pallas_call x1, Pallas kernels: 64.1 us -> 62.7 us  [local(): pl.pallas_call(kernel, out_shape=jax.ShapeDtypeStruct((OWN, NB * BLK), F3...]
where the time goes in v5:
time: 64.3 us; the launch traced here: 64.1 us
  Pallas kernels  62.7 us (98%)
  local copies, waits for them, and re-layouts  1.47 us (2%)
    pallas_call x1, Pallas kernels, local(): pl.pallas_call(kernel, out_shape=jax.ShapeDtypeStruct((OWN, NB * BLK), F3...  62.7 us
    unnamed x1, local copies, waits for them, and re-layouts  1.47 us

profile of v5, /device:TPU:1, one launch (start us, length us, event | category | flops | bytes accessed | tf_op | source)
XLA Modules:
  0.0 64.1 jit_solution(12941426619917417196)
XLA Ops:
  0.0 62.7 %precondition.1 = f32[4,4096]{1,0:T(4,128)} custom-call(f32[4,4096]{1,0:T(4,128)} %states_hbm.1, bf16[32,3,128,128]{3,2,1,0:T(8,128)(2,1)} %w_hbm.1, s32[3,32]{1,0:T(4,128)} %bitcast.1, s32[32]{0:T(128)} %partner_hbm.1), custom_call_target="tpu_custom_call" | custom-call | tf_op jit(solution)/shard_map/precondition/pallas_call | solution.py:408
  62.7 1.5 %copy.6 = f32[4,4096]{1,0:T(4,128)} copy(f32[4,4096]{1,0:T(4,128)} %precondition.1) | data formatting | bytes 131072

commit v6 on v5

--- a/solution.py
+++ b/solution.py
@@ -183,22 +183,23 @@
 
     mine = x * 2 + core
 
-    def sum_start(value, phase):
+    def sum_start(value, phase, which):
         buf, place_here, device = (
             (pack_c, c, lambda a: {"cols": a}),
             (pack_a, mine, lambda a: {"rows": (a // 2) * 16 + z * 2 + lax.rem(a, 2)}),
             (pack_b, z, lambda a: {"rows": x * 16 + a * 2 + core}),
         )[phase]
+        buf, n = buf.at[which], 3 * which + phase
         buf[place_here] = value
         for j in range(1, 8):
-            rcopy(buf.at[place_here], buf.at[place_here], sum_send.at[phase], sum_recv.at[phase],
+            rcopy(buf.at[place_here], buf.at[place_here], sum_send.at[n], sum_recv.at[n],
                   device(lax.rem(place_here + ORDER[j - 1], 8))).start()
-        ends.append(lambda: wait_bytes(buf.at[pl.ds(0, 7)], sum_send.at[phase]))
-        open_waits["sum", phase] = lambda: wait_bytes(buf.at[pl.ds(0, 7)], sum_recv.at[phase])
-
-    def sum_end(phase):
-        buf = (pack_c, pack_a, pack_b)[phase]
-        wait("sum", phase)
+        ends.append(lambda: wait_bytes(buf.at[pl.ds(0, 7)], sum_send.at[n]))
+        open_waits["sum", n] = lambda: wait_bytes(buf.at[pl.ds(0, 7)], sum_recv.at[n])
+
+    def sum_end(phase, which):
+        buf = (pack_c, pack_a, pack_b)[phase].at[which]
+        wait("sum", 3 * which + phase)
         return ((buf[0] + buf[1]) + (buf[2] + buf[3])) + ((buf[4] + buf[5]) + (buf[6] + buf[7]))
 
     halo(ext_y, 0)
@@ -236,37 +237,39 @@
     slot_copy.wait()
     lt[pl.ds(4 * c, 4)] = appl[pl.ds(4 * c, 4)]
     pair(coarse, send_2, arr_2, 0)
-    own_pass(ext_z)
+
     def column(ref, u):
         return jnp.concatenate([ref[4 * m + u] for m in range(NC)], axis=0)
 
     def packed_parts(block):
         return jnp.concatenate(parts(block), axis=0).astype(BF16)
 
-    wait("turn", 0)
-    wait("turn", 1)
-    pad = jnp.zeros((32, BLK), BF16)
-    left, right_g, right_r = [], [], []
-    for u in range(4):
-        block = column(yt, u)
-        packed = packed_parts(block)
-        lparts[u] = packed
-        left.append(packed)
-        weighted = block * jnp.broadcast_to(deg[4 * c + u][0:1], (COLS, BLK))
-        right_g.append(jnp.concatenate([packed_parts(weighted), pad], axis=0))
-        right_r.append(jnp.concatenate([packed_parts(column(lt, u)), pad], axis=0))
-    left = jnp.concatenate(left, axis=1)
     lane = lanes((8, 128))
-    pieces = []
-    for right in (right_g, right_r):
-        total = lax.dot_general(left, jnp.concatenate(right, axis=1), NT, preferred_element_type=F32)
+
+    def small_product(right):
+        pad = jnp.zeros((32, BLK), BF16)
+        left = jnp.concatenate([lparts[u] for u in range(4)], axis=1)
+        right = jnp.concatenate([jnp.concatenate([piece, pad], axis=0) for piece in right], axis=1)
+        total = lax.dot_general(left, right, NT, preferred_element_type=F32)
         total = total[0:32] + total[32:64] + total[64:96]
         total = total + pltpu.roll(total, 128 - 32, 1) + pltpu.roll(total, 128 - 64, 1)
         piece = jnp.where(lane < 32, total[0:8], 0.0)
         for g in range(1, 4):
             piece += pltpu.roll(jnp.where(lane < 32, total[8 * g:8 * g + 8], 0.0), 32 * g, 1)
-        pieces.append(piece)
-    sum_start(jnp.concatenate(pieces, axis=0), 0)
+        return piece
+
+    wait("turn", 0)
+    weighted = []
+    for u in range(4):
+        block = column(yt, u)
+        lparts[u] = packed_parts(block)
+        weighted.append(packed_parts(block * jnp.broadcast_to(deg[4 * c + u][0:1], (COLS, BLK))))
+    sum_start(small_product(weighted), 0, 0)
+    own_pass(ext_z)
+    wait("turn", 1)
+    packed_r = small_product([packed_parts(column(lt, u)) for u in range(4)])
+    sum_start(packed_r, 0, 1)
+    sum_start(sum_end(0, 0), 1, 0)
     wait("halo", 1)
 
     def after_z(b, neighbour, _):
@@ -289,8 +292,9 @@
         rcopy(coarse, gathered.at[c], turn_send.at[2], turn_recv.at[2], {"cols": peer}).start()
     ends.append(lambda: wait_bytes(gathered.at[pl.ds(0, 7)], turn_send.at[2]))
     open_waits["turn", 2] = lambda: wait_bytes(gathered.at[pl.ds(0, 7)], turn_recv.at[2])
-    sum_start(sum_end(0), 1)
-    sum_start(sum_end(1), 2)
+    sum_start(sum_end(0, 1), 1, 1)
+    sum_start(sum_end(1, 0), 2, 0)
+    sum_start(sum_end(1, 1), 2, 1)
     wait("pair", 1)
 
     def meet_fine(b):
@@ -299,12 +303,13 @@
         cdeg[b] = DAMP / (deg[b] + jnp.broadcast_to(got[OWN:OWN + 1], (OWN, BLK)))
 
     blocks(meet_fine)
-    packed = sum_end(2)
+    packed_g = sum_end(2, 0)
+    packed_r = sum_end(2, 1)
 
     rows_g, rows_r = [], []
     for g in range(4):
-        piece = pltpu.roll(packed[0:8], 128 - 32 * g, 1) if g else packed[0:8]
-        other = pltpu.roll(packed[8:16], (160 - 32 * g) % 128, 1) if g != 1 else packed[8:16]
+        piece = pltpu.roll(packed_g, 128 - 32 * g, 1) if g else packed_g
+        other = pltpu.roll(packed_r, (160 - 32 * g) % 128, 1) if g != 1 else packed_r
         rows_g.append(jnp.where(lane < 32, piece, jnp.where(lane < 64, other, 0.0)))
     matrix = jnp.concatenate(rows_g, axis=0)
     lane32 = lanes((COLS, 128))
@@ -403,7 +408,7 @@
     extended = pltpu.VMEM((NB + 2 * HB, OWN, BLK), F32)
     slots = pltpu.VMEM((NR, OWN, BLK), F32)
     slots_2 = pltpu.VMEM((NR, OWN + 1, BLK), F32)
-    packs = pltpu.VMEM((8, 16, 128), F32)
+    packs = pltpu.VMEM((2, 8, 8, 128), F32)
     dma = pltpu.SemaphoreType.DMA
     return pl.pallas_call(
         kernel,
@@ -426,7 +431,7 @@
             pltpu.VMEM((NR, 1, BLK), F32),
             pltpu.VMEM((1, 128), jnp.int32), pltpu.SMEM((1, 128), jnp.int32),
             dma((3,)), dma((3,)), dma, dma((4, 2)), dma((4, 2)), dma((5,)), dma((5,)), dma((4,)), dma((4,)),
-            dma((3,)), dma((3,)),
+            dma((6,)), dma((6,)),
         ],
         compiler_params=pltpu.CompilerParams(
             collective_id=0, has_side_effects=True, vmem_limit_bytes=60 * 1024 * 1024

time: 64.3 us -> 63.8 us (level)
  no operation moved by 1% of the time
where the time goes in v6:
time: 63.8 us; the launch traced here: 63.7 us
  Pallas kernels  62.2 us (97%)
  local copies, waits for them, and re-layouts  1.47 us (2%)
    pallas_call x1, Pallas kernels, local(): pl.pallas_call(kernel, out_shape=jax.ShapeDtypeStruct((OWN, NB * BLK), F3...  62.2 us
    unnamed x1, local copies, waits for them, and re-layouts  1.47 us

profile of v6, /device:TPU:1, one launch (start us, length us, event | category | flops | bytes accessed | tf_op | source)
XLA Modules:
  0.0 63.7 jit_solution(15182146319978458546)
XLA Ops:
  0.0 62.2 %precondition.1 = f32[4,4096]{1,0:T(4,128)} custom-call(f32[4,4096]{1,0:T(4,128)} %states_hbm.1, bf16[32,3,128,128]{3,2,1,0:T(8,128)(2,1)} %w_hbm.1, s32[3,32]{1,0:T(4,128)} %bitcast.1, s32[32]{0:T(128)} %partner_hbm.1), custom_call_target="tpu_custom_call" | custom-call | tf_op jit(solution)/shard_map/precondition/pallas_call | solution.py:413
  62.2 1.5 %copy.6 = f32[4,4096]{1,0:T(4,128)} copy(f32[4,4096]{1,0:T(4,128)} %precondition.1) | data formatting | bytes 131072
